TPU v7x, 32 devices: a whole 2x2x4 slice. The times are simulated.
32 devices in a mesh: dp: 8 (over y, x, core), tensor: 4 (over z).
Axes of the slice: x: 2, y: 2, z: 4, core: 2. Of those that a mesh axis runs over, the one named last changes fastest.
Arguments:
- inputs: bfloat16 [16384, 1024], P(('dp', 'tensor')), may hold values from -6 to 6
- cotangent: bfloat16 [16384, 1024], P(('dp', 'tensor')), may hold values from -6 to 6
- seq_lens: int32 [8, 64], P('dp'), may hold values from 0 to 512, as said below
- gains: float32 [2, 1024], P(None, 'dp'), may hold values from 0.5 to 1.5
- w_qkv: float32 [3, 1024, 1024], P(None, 'dp', 'tensor'), may hold values from -0.1875 to 0.1875
- w_out: float32 [1024, 1024], P('tensor', 'dp'), may hold values from -1 to 1
- w_in: float32 [2, 1024, 2624], P(None, 'dp', 'tensor'), may hold values from -0.1875 to 0.1875
- w_down: float32 [2624, 1024], P('tensor', 'dp'), may hold values from -0.125 to 0.125
- moment_gains: float32 [2, 1024], P(None, 'dp'), may hold values from -64 to 64
- square_gains: float32 [2, 1024], P(None, 'dp'), may hold values from 116.98176 to 1871.7081
- moment_qkv: float32 [3, 1024, 1024], P(None, 'dp', 'tensor'), may hold values from -32 to 32
- square_qkv: float32 [3, 1024, 1024], P(None, 'dp', 'tensor'), may hold values from 29.24544 to 467.92703
- moment_out: float32 [1024, 1024], P('tensor', 'dp'), may hold values from -8 to 8
- square_out: float32 [1024, 1024], P('tensor', 'dp'), may hold values from 1.6845373 to 26.952597
- moment_in: float32 [2, 1024, 2624], P(None, 'dp', 'tensor'), may hold values from -28 to 28
- square_in: float32 [2, 1024, 2624], P(None, 'dp', 'tensor'), may hold values from 18.717081 to 299.4733
- moment_down: float32 [2624, 1024], P('tensor', 'dp'), may hold values from -48 to 48
- square_down: float32 [2624, 1024], P('tensor', 'dp'), may hold values from 49.13234 to 786.11743
Outputs:
- outputs: float32 [16384, 1024], P(('dp', 'tensor'))
- grad_inputs: float32 [16384, 1024], P(('dp', 'tensor'))
- new_moment_gains: float32 [2, 1024], P(None, 'dp')
- new_square_gains: float32 [2, 1024], P(None, 'dp')
- new_gains: float32 [2, 1024], P(None, 'dp')
- new_moment_qkv: float32 [3, 1024, 1024], P(None, 'dp', 'tensor')
- new_square_qkv: float32 [3, 1024, 1024], P(None, 'dp', 'tensor')
- new_qkv: float32 [3, 1024, 1024], P(None, 'dp', 'tensor')
- new_moment_out: float32 [1024, 1024], P('tensor', 'dp')
- new_square_out: float32 [1024, 1024], P('tensor', 'dp')
- new_out: float32 [1024, 1024], P('tensor', 'dp')
- new_moment_in: float32 [2, 1024, 2624], P(None, 'dp', 'tensor')
- new_square_in: float32 [2, 1024, 2624], P(None, 'dp', 'tensor')
- new_in: float32 [2, 1024, 2624], P(None, 'dp', 'tensor')
- new_moment_down: float32 [2624, 1024], P('tensor', 'dp')
- new_square_down: float32 [2624, 1024], P('tensor', 'dp')
- new_down: float32 [2624, 1024], P('tensor', 'dp')
Inputs may be any that keep to these rules, and one draw needn't show every extreme that they name: `seq_lens`: row g lists the lengths of data group g's sequences in their order in the group; used slots come first and the rest are 0; slot 0 holds a sequence of exactly 512; a row sums to at most 2048 and to at least 512.
All inputs are finite; a program needn't handle non-finite values.
Results may differ from a plain program's by a relative error of at most 0.013.
The roundings to bfloat16 on the way count: a program that leaves them out, or rounds other values in their place, can miss the bound.
Values may be sent and summed in bfloat16 or wider, within the bound.
A program may use at most 128 MiB of HBM per device.

v0:
```python
import jax
import jax.numpy as jnp
from jax import lax
from jax.sharding import PartitionSpec as P

MAXLEN = 512
QBLOCK = 512
STEP = 10
HEAD_DIM = 64


NORM_EPS = 1e-05
ROPE_BASE = 160000.0
NEG_LARGE = -1000000000.0
BETA_ONE = 0.9
BETA_TWO = 0.98
ADAM_EPS = 1e-06
LEARN_RATE = 0.05
GAIN_RATE = 0.2
WEIGHT_DECAY = 0.01


def layout(lengths, count):
    ends = jnp.cumsum(lengths)
    starts = ends - lengths
    row_ids = jnp.arange(count, dtype=jnp.int32)
    member = (row_ids[:, None] >= starts[None, :]) & (row_ids[:, None] < ends[None, :])
    slot_ids = jnp.arange(lengths.shape[0], dtype=jnp.int32)
    valid = jnp.any(member, axis=1)
    segment = jnp.where(valid, jnp.sum(jnp.where(member, slot_ids[None, :], 0), axis=1), -1)
    position = row_ids - jnp.sum(jnp.where(member, starts[None, :], 0), axis=1)
    return (segment, position, valid)


def rotary(values, position):
    head_size = values.shape[-1]
    half_size = head_size // 2
    exponents = jnp.arange(half_size, dtype=jnp.float32) * (2.0 / head_size)
    frequency = ROPE_BASE ** (-exponents)
    angles = position.astype(jnp.float32)[:, None] * frequency[None, :]
    cosine_table = jnp.concatenate([jnp.cos(angles), jnp.cos(angles)], axis=-1)[:, None, :]
    sine_table = jnp.concatenate([jnp.sin(angles), jnp.sin(angles)], axis=-1)[:, None, :]
    rotated = jnp.concatenate([-values[..., half_size:], values[..., :half_size]], axis=-1)
    return values * cosine_table + rotated * sine_table


def normalize(values):
    centered = values - jnp.mean(values, axis=-1, keepdims=True)
    inverse = lax.rsqrt(jnp.mean(centered * centered, axis=-1, keepdims=True) + NORM_EPS)
    return (centered * inverse, inverse)


def norm_back(grad_normed, normed, inverse):
    first_mean = jnp.mean(grad_normed, axis=-1, keepdims=True)
    second_mean = jnp.mean(grad_normed * normed, axis=-1, keepdims=True)
    return inverse * (grad_normed - first_mean - normed * second_mean)


def allowed_mask(query_segment, query_index, key_segment, key_index):
    same = (query_segment[:, None] == key_segment[None, :]) & (query_segment[:, None] >= 0)
    return same | (query_index[:, None] == key_index[None, :])


def block_scores(queries, pad_keys, segment, pad_segment, pad_index, start, block, window):
    scale = queries.shape[-1] ** (-0.5)
    query_block = lax.dynamic_slice_in_dim(queries, start, block, 0)
    key_block = lax.dynamic_slice_in_dim(pad_keys, start, window, 0)
    query_segment = lax.dynamic_slice_in_dim(segment, start, block, 0)
    query_index = start + jnp.arange(block, dtype=jnp.int32)
    key_segment = lax.dynamic_slice_in_dim(pad_segment, start, window, 0)
    key_index = lax.dynamic_slice_in_dim(pad_index, start, window, 0)
    scores = (
        jnp.einsum("qhd,khd->hqk", query_block, key_block, preferred_element_type=jnp.float32)
        * scale
    )
    allowed = allowed_mask(query_segment, query_index, key_segment, key_index)
    return (jnp.where(allowed[None], scores, NEG_LARGE), query_block, key_block)


def padded_tables(keys, values, segment, margin):
    total = keys.shape[0]
    pad_keys = jnp.pad(keys, ((margin, margin), (0, 0), (0, 0)))
    pad_values = jnp.pad(values, ((margin, margin), (0, 0), (0, 0)))
    pad_segment = jnp.pad(segment, (margin, margin), constant_values=-1)
    pad_index = jnp.arange(total + 2 * margin, dtype=jnp.int32) - margin
    return (pad_keys, pad_values, pad_segment, pad_index)


def attend_forward(queries, keys, values, segment, block, margin):
    total = queries.shape[0]
    window = block + 2 * margin
    pad_keys, pad_values, pad_segment, pad_index = padded_tables(keys, values, segment, margin)

    def one_block(number):
        start = number * block
        scores, query_block, key_block = block_scores(
            queries, pad_keys, segment, pad_segment, pad_index, start, block, window
        )
        value_block = lax.dynamic_slice_in_dim(pad_values, start, window, 0)
        top = jnp.max(scores, axis=-1, keepdims=True)
        log_total = top + jnp.log(jnp.sum(jnp.exp(scores - top), axis=-1, keepdims=True))
        weights = jnp.exp(scores - log_total).astype(jnp.bfloat16)
        mixed = jnp.einsum("hqk,khd->qhd", weights, value_block, preferred_element_type=jnp.float32)
        return (mixed.astype(jnp.bfloat16), log_total)

    mixed, log_totals = lax.map(one_block, jnp.arange(total // block, dtype=jnp.int32))
    return (mixed.reshape(total, -1), log_totals)


def attend_backward(queries, keys, values, grad_mixed, log_totals, segment, block, margin):
    total = queries.shape[0]
    window = block + 2 * margin
    scale = queries.shape[-1] ** (-0.5)
    pad_keys, pad_values, pad_segment, pad_index = padded_tables(keys, values, segment, margin)

    def one_block(carry, number):
        grad_keys, grad_values = carry
        start = number * block
        scores, query_block, key_block = block_scores(
            queries, pad_keys, segment, pad_segment, pad_index, start, block, window
        )
        value_block = lax.dynamic_slice_in_dim(pad_values, start, window, 0)
        probs = jnp.exp(scores - log_totals[number])
        weights = probs.astype(jnp.bfloat16)
        grad_block = lax.dynamic_slice_in_dim(grad_mixed, start, block, 0)
        grad_probs = jnp.einsum(
            "qhd,khd->hqk", grad_block, value_block, preferred_element_type=jnp.float32
        )
        inner = jnp.sum(probs * grad_probs, axis=-1, keepdims=True)
        grad_scores = (probs * (grad_probs - inner)).astype(jnp.bfloat16)
        grad_query = (
            jnp.einsum("hqk,khd->qhd", grad_scores, key_block, preferred_element_type=jnp.float32)
            * scale
        )
        key_part = (
            jnp.einsum("hqk,qhd->khd", grad_scores, query_block, preferred_element_type=jnp.float32)
            * scale
        )
        value_part = jnp.einsum(
            "hqk,qhd->khd", weights, grad_block, preferred_element_type=jnp.float32
        )
        grad_keys = lax.dynamic_update_slice_in_dim(
            grad_keys, lax.dynamic_slice_in_dim(grad_keys, start, window, 0) + key_part, start, 0
        )
        grad_values = lax.dynamic_update_slice_in_dim(
            grad_values,
            lax.dynamic_slice_in_dim(grad_values, start, window, 0) + value_part,
            start,
            0,
        )
        return ((grad_keys, grad_values), grad_query)

    zeros = jnp.zeros((total + 2 * margin,) + keys.shape[1:], jnp.float32)
    (grad_keys, grad_values), grad_queries = lax.scan(
        one_block, (zeros, zeros), jnp.arange(total // block, dtype=jnp.int32)
    )
    return (
        grad_queries.reshape(queries.shape),
        grad_keys[margin : margin + total],
        grad_values[margin : margin + total],
    )


def adam_step(param, grad, moment, square, rate, decay):
    moment = BETA_ONE * moment + (1.0 - BETA_ONE) * grad
    square = BETA_TWO * square + (1.0 - BETA_TWO) * grad * grad
    moment_hat = moment / (1.0 - BETA_ONE**STEP)
    square_hat = square / (1.0 - BETA_TWO**STEP)
    updated = param - rate * (moment_hat / (jnp.sqrt(square_hat) + ADAM_EPS) + decay * param)
    return (moment, square, updated)


def gated(pre_part, gate_part):
    return jax.nn.gelu(pre_part, approximate=False) * gate_part


def body(
    inputs,
    cotangent,
    seq_lens,
    gains,
    w_qkv,
    w_out,
    w_in,
    w_down,
    moment_gains,
    square_gains,
    moment_qkv,
    square_qkv,
    moment_out,
    square_out,
    moment_in,
    square_in,
    moment_down,
    square_down,
):
    local_rows = inputs.shape[0]
    group_rows = local_rows * lax.axis_size("tensor")
    my_start = lax.axis_index("tensor") * local_rows
    gains_all, qkv_all, proj_all, expand_all, reduce_all = (
        lax.all_gather(gains.astype(jnp.bfloat16), "dp", axis=1, tiled=True),
        lax.all_gather(w_qkv.astype(jnp.bfloat16), "dp", axis=1, tiled=True),
        lax.all_gather(w_out.astype(jnp.bfloat16), "dp", axis=1, tiled=True),
        lax.all_gather(w_in.astype(jnp.bfloat16), "dp", axis=1, tiled=True),
        lax.all_gather(w_down.astype(jnp.bfloat16), "dp", axis=1, tiled=True),
    )
    gain_values = gains_all.astype(jnp.float32)
    segment, position, valid = layout(seq_lens[0], group_rows)
    my_valid = lax.dynamic_slice_in_dim(valid, my_start, local_rows, 0).astype(jnp.float32)
    head_size = HEAD_DIM
    local_heads = qkv_all.shape[2] // head_size
    residual = inputs.astype(jnp.float32)
    normed_one, inverse_one = normalize(residual)
    first_rows = lax.all_gather(
        (normed_one * gain_values[0]).astype(jnp.bfloat16), "tensor", axis=0, tiled=True
    )
    projected = jnp.einsum("rd,kdc->krc", first_rows, qkv_all, preferred_element_type=jnp.float32)
    query_raw = projected[0].reshape(group_rows, local_heads, head_size)
    key_raw = projected[1].reshape(group_rows, local_heads, head_size)
    queries = rotary(query_raw, position).astype(jnp.bfloat16)
    keys = rotary(key_raw, position).astype(jnp.bfloat16)
    values = projected[2].reshape(group_rows, local_heads, head_size).astype(jnp.bfloat16)
    attended, log_totals = attend_forward(queries, keys, values, segment, QBLOCK, MAXLEN)
    middle = residual + lax.psum_scatter(
        jnp.dot(attended, proj_all, preferred_element_type=jnp.float32),
        "tensor",
        scatter_dimension=0,
        tiled=True,
    )
    normed_two, inverse_two = normalize(middle)
    second_rows = lax.all_gather(
        (normed_two * gain_values[1]).astype(jnp.bfloat16), "tensor", axis=0, tiled=True
    )
    expanded = jnp.einsum(
        "rd,kdf->krf", second_rows, expand_all, preferred_element_type=jnp.float32
    )
    hidden_full, gated_back = jax.vjp(gated, expanded[0], expanded[1])
    hidden = hidden_full.astype(jnp.bfloat16)
    outputs = middle + lax.psum_scatter(
        jnp.dot(hidden, reduce_all, preferred_element_type=jnp.float32).astype(jnp.bfloat16),
        "tensor",
        scatter_dimension=0,
        tiled=True,
    ).astype(jnp.float32)
    grad_masked = cotangent.astype(jnp.float32) * my_valid[:, None]
    grad_rows = lax.all_gather(grad_masked.astype(jnp.bfloat16), "tensor", axis=0, tiled=True)
    grad_reduce = jnp.einsum("rf,rd->fd", hidden, grad_rows, preferred_element_type=jnp.float32)
    grad_hidden = jnp.einsum("rd,fd->rf", grad_rows, reduce_all, preferred_element_type=jnp.float32)
    grad_pre, grad_gate = gated_back(grad_hidden)
    grad_expanded = jnp.stack([grad_pre, grad_gate]).astype(jnp.bfloat16)
    grad_expand = jnp.einsum(
        "rd,krf->kdf", second_rows, grad_expanded, preferred_element_type=jnp.float32
    )
    grad_second = lax.psum_scatter(
        jnp.einsum("krf,kdf->rd", grad_expanded, expand_all, preferred_element_type=jnp.float32),
        "tensor",
        scatter_dimension=0,
        tiled=True,
    )
    gain_two = jnp.sum(grad_second * normed_two, axis=0)
    grad_middle = grad_masked + norm_back(grad_second * gain_values[1], normed_two, inverse_two)
    middle_rows = lax.all_gather(grad_middle.astype(jnp.bfloat16), "tensor", axis=0, tiled=True)
    grad_proj = jnp.einsum("rc,rd->cd", attended, middle_rows, preferred_element_type=jnp.float32)
    grad_attended = jnp.einsum(
        "rd,cd->rc", middle_rows, proj_all, preferred_element_type=jnp.float32
    )
    grad_attended = grad_attended.astype(jnp.bfloat16).reshape(group_rows, local_heads, head_size)
    grad_queries, grad_keys, grad_values = attend_backward(
        queries, keys, values, grad_attended, log_totals, segment, QBLOCK, MAXLEN
    )

    def rope_at(angles_input):
        return rotary(angles_input, position)

    unused, rope_back = jax.vjp(rope_at, query_raw)
    grad_projected = jnp.stack(
        [
            rope_back(grad_queries)[0].reshape(group_rows, -1),
            rope_back(grad_keys)[0].reshape(group_rows, -1),
            grad_values.reshape(group_rows, -1),
        ]
    ).astype(jnp.bfloat16)
    grad_qkv = jnp.einsum(
        "rd,krc->kdc", first_rows, grad_projected, preferred_element_type=jnp.float32
    )
    grad_first = lax.psum_scatter(
        jnp.einsum(
            "krc,kdc->rd", grad_projected, qkv_all, preferred_element_type=jnp.float32
        ).astype(jnp.bfloat16),
        "tensor",
        scatter_dimension=0,
        tiled=True,
    ).astype(jnp.float32)
    gain_one = jnp.sum(grad_first * normed_one, axis=0)
    grad_inputs = grad_middle + norm_back(grad_first * gain_values[0], normed_one, inverse_one)
    gain_terms = jnp.stack([gain_one, gain_two])
    gain_share, qkv_sum, proj_sum, expand_sum, reduce_sum = (
        lax.psum_scatter(gain_terms, "dp", scatter_dimension=1, tiled=True),
        lax.psum_scatter(grad_qkv, "dp", scatter_dimension=1, tiled=True),
        lax.psum_scatter(grad_proj, "dp", scatter_dimension=1, tiled=True),
        lax.psum_scatter(grad_expand, "dp", scatter_dimension=1, tiled=True),
        lax.psum_scatter(grad_reduce, "dp", scatter_dimension=1, tiled=True),
    )
    gain_grads = lax.psum(gain_share, "tensor")
    gains_new = adam_step(gains, gain_grads, moment_gains, square_gains, GAIN_RATE, 0.0)
    qkv_new = adam_step(w_qkv, qkv_sum, moment_qkv, square_qkv, LEARN_RATE, WEIGHT_DECAY)
    out_new = adam_step(w_out, proj_sum, moment_out, square_out, LEARN_RATE, WEIGHT_DECAY)
    in_new = adam_step(w_in, expand_sum, moment_in, square_in, LEARN_RATE, WEIGHT_DECAY)
    down_new = adam_step(w_down, reduce_sum, moment_down, square_down, LEARN_RATE, WEIGHT_DECAY)
    return (
        outputs,
        grad_inputs,
        gains_new[0],
        gains_new[1],
        gains_new[2],
        qkv_new[0],
        qkv_new[1],
        qkv_new[2],
        out_new[0],
        out_new[1],
        out_new[2],
        in_new[0],
        in_new[1],
        in_new[2],
        down_new[0],
        down_new[1],
        down_new[2],
    )


def solution(mesh):
    in_specs = (
        P(("dp", "tensor"), None),
        P(("dp", "tensor"), None),
        P("dp", None),
        P(None, "dp"),
        P(None, "dp", "tensor"),
        P("tensor", "dp"),
        P(None, "dp", "tensor"),
        P("tensor", "dp"),
        P(None, "dp"),
        P(None, "dp"),
        P(None, "dp", "tensor"),
        P(None, "dp", "tensor"),
        P("tensor", "dp"),
        P("tensor", "dp"),
        P(None, "dp", "tensor"),
        P(None, "dp", "tensor"),
        P("tensor", "dp"),
        P("tensor", "dp"),
    )
    out_specs = (
        P(("dp", "tensor"), None),
        P(("dp", "tensor"), None),
        P(None, "dp"),
        P(None, "dp"),
        P(None, "dp"),
        P(None, "dp", "tensor"),
        P(None, "dp", "tensor"),
        P(None, "dp", "tensor"),
        P("tensor", "dp"),
        P("tensor", "dp"),
        P("tensor", "dp"),
        P(None, "dp", "tensor"),
        P(None, "dp", "tensor"),
        P(None, "dp", "tensor"),
        P("tensor", "dp"),
        P("tensor", "dp"),
        P("tensor", "dp"),
    )
    return jax.shard_map(body, mesh=mesh, in_specs=in_specs, out_specs=out_specs, check_vma=False)
```

profile of v0, /device:TPU:0, one launch (start us, length us, event | category | flops | bytes accessed | tf_op | source)
XLA Modules:
  0.0 1322.3 jit_solution(16145848899268102183)
XLA Ops:
  10.0 10.2 all_gather.27
  24.5 10.9 all_gather.30
  39.6 83.2 %all-gather.8.cloned.1.call-done = bf16[2048,1024]{1,0:T(8,128)(2,1)} async-done(((bf16[512,1024]{1,0:T(8,128)(2,1)}), bf16[2048,1024]{1,0:T(8,128)(2,1)}) %all-gather.8.cloned.1.call-update) | async-done | bytes 4194320 | tf_op jit(solution)/shard_map/all_gather | solution.py:214
  133.5 58.7 %while.26 = (s32[]{:T(128)}, bf16[4,512,4,64]{1,3,2,0:T(8,128)(2,1)}, f32[4,4,512,1]{2,1,3,0:T(4,128)S(1)}, s32[4]{0:T(128)S(1)}, bf16[3072,4,64]{0,2,1:T(8,128)...) while((s32[]{:T(128)}, ...), condition=%wide.region_9.10_spmd, body=%wide.region_6.9_spmd.sunk | while | flops 843185152 | bytes 43105548 | solution.py:106
  205.9 137.4 %reduce-scatter.12.cloned.1.call-done = f32[512,1024]{1,0:T(8,128)} async-done(((f32[2048,1024]{1,0:T(8,128)}), f32[512,1024]{1,0:T(8,128)}) %reduce-scatter.12.cloned.1.call-update) | async-done | bytes 2097168 | tf_op jit(solution)/shard_map/reduce_scatter | solution.py:224
  347.9 23.4 %all-gather.16.cloned.1.call-done = bf16[656,1024]{1,0:T(8,128)(2,1)} async-done(((bf16[656,128]{1,0:T(8,128)(2,1)}), bf16[656,1024]{1,0:T(8,128)(2,1)}) %all-gather.16.cloned.1.call-update) | async-done | bytes 1343504 | tf_op jit(solution)/shard_map/all_gather | solution.py:205
  371.3 82.8 %all-gather.18.cloned.1.call-done = bf16[2048,1024]{1,0:T(8,128)(2,1)} async-done(((bf16[512,1024]{1,0:T(8,128)(2,1)}), bf16[2048,1024]{1,0:T(8,128)(2,1)}) %all-gather.18.cloned.1.call-update) | async-done | bytes 4194320 | tf_op jit(solution)/shard_map/all_gather | solution.py:246
  462.0 23.8 %all-gather.14.cloned.1.call-done = bf16[2,1024,656]{1,2,0:T(8,128)(2,1)} async-done(((bf16[2,128,656]{1,2,0:T(8,128)(2,1)}), bf16[2,1024,656]{1,2,0:T(8,128)(2,1)}) %all-gather.14.cloned.1.call-update) | async-done | bytes 2686992 | tf_op jit(solution)/shard_map/all_gather | solution.py:204
  485.7 82.4 %all-gather.12.cloned.1.call-done = bf16[2048,1024]{1,0:T(8,128)(2,1)} async-done(((bf16[512,1024]{1,0:T(8,128)(2,1)}), bf16[2048,1024]{1,0:T(8,128)(2,1)}) %all-gather.12.cloned.1.call-update) | async-done | bytes 4194320 | tf_op jit(solution)/shard_map/all_gather | solution.py:231
  576.7 13.7 %fusion.73 = (bf16[1,2048,656]{1,2,0:T(8,128)(2,1)}, f32[2048,656]{0,1:T(8,128)S(1)}) fusion(f32[2048,656]{0,1:T(8,128)S(1)} %copy-done.6, f32[2,2048,656]{1,2,0:T(8,128)S(1)} %convolution_bitcast_fusion), kind=kLoop, calls=%fused_computation.103 | loop fusion | flops 98074624 | bytes 24182784 | tf_op jit(solution)/shard_map/stack | solution.py:250
  594.5 12.1 convolution_bitcast_fusion.1
  614.5 135.3 %reduce-scatter.16.cloned.1.call-done = f32[512,1024]{1,0:T(8,128)} async-done(((f32[2048,1024]{1,0:T(8,128)}), f32[512,1024]{1,0:T(8,128)}) %reduce-scatter.16.cloned.1.call-update) | async-done | bytes 2097168 | tf_op jit(solution)/shard_map/reduce_scatter | solution.py:254
  753.4 76.2 %reduce-scatter.14.cloned.1.call-done = bf16[512,1024]{1,0:T(8,128)(2,1)} async-done(((bf16[2048,1024]{1,0:T(8,128)(2,1)}), bf16[512,1024]{1,0:T(8,128)(2,1)}) %reduce-scatter.14.cloned.1.call-update) | async-done | bytes 1048592 | tf_op jit(solution)/shard_map/reduce_scatter | solution.py:239
  841.8 11.0 fusion.81
  852.9 62.8 %all-gather.20.cloned.1.call-done = bf16[2048,1024]{1,0:T(8,128)(2,1)} async-done(((bf16[512,1024]{1,0:T(8,128)(2,1)}), bf16[2048,1024]{1,0:T(8,128)(2,1)}) %all-gather.20.cloned.1.call-update) | async-done | bytes 4194320 | tf_op jit(solution)/shard_map/all_gather | solution.py:262
  924.2 163.0 %while.27 = (s32[]{:T(128)}, f32[3072,4,64]{0,2,1:T(8,128)}, f32[3072,4,64]{0,2,1:T(8,128)}, f32[4,512,4,64]{1,0,3,2:T(4,128)}, s32[4]{0:T(128)S(1)}, /*index=5*...) while((s32[]{:T(128)}, f32[3072,4,64]{0,2,1:T(8,128)}, ...), condition=%wide.region_19.20_spmd, body=%wide.region_17.19_spmd.sunk | while | flops 2046032896 | bytes 146103760 | solution.py:154
  954.1 11.1 dynamic_update_slice.31
  995.1 11.1 dynamic_update_slice.31
  1035.6 11.1 dynamic_update_slice.31
  1076.2 11.1 dynamic_update_slice.31
  1139.0 46.1 %reduce-scatter.20.cloned.1.call-done = f32[3,128,256]{1,2,0:T(8,128)} async-done(((f32[3,1024,256]{1,2,0:T(8,128)}), f32[3,128,256]{1,2,0:T(8,128)}) %reduce-scatter.20.cloned.1.call-update) | async-done | bytes 393232 | tf_op jit(solution)/shard_map/reduce_scatter | solution.py:299
  1192.1 71.9 %reduce-scatter.18.cloned.1.call-done = bf16[512,1024]{1,0:T(8,128)(2,1)} async-done(((bf16[2048,1024]{1,0:T(8,128)(2,1)}), bf16[512,1024]{1,0:T(8,128)(2,1)}) %reduce-scatter.18.cloned.1.call-update) | async-done | bytes 1048592 | tf_op jit(solution)/shard_map/reduce_scatter | solution.py:286
  1270.6 31.5 %reduce-scatter.28.cloned.1.call-done = f32[128,2]{1,0:T(8,128)} async-done(((f32[1024,2]{1,0:T(8,128)}), f32[128,2]{1,0:T(8,128)}) %reduce-scatter.28.cloned.1.call-update) | async-done | bytes 1040
  1303.0 11.7 psum.7
  (318 shorter events, 323.2 us)
Async XLA Ops:
  7.2 32.4 %all-gather.10.cloned.1.call-start = ((), (), s32[]{:S(2)}) async-start(), calls=%async_computation.10 | async-start | bytes 1769472 | tf_op jit(solution)/shard_map/all_gather | solution.py:202
  9.2 113.5 %all-gather.8.cloned.1.call-start = ((), (), s32[]{:S(2)}) async-start(), calls=%async_computation.9 | async-start | bytes 5242880 | tf_op jit(solution)/shard_map/all_gather | solution.py:214
  23.5 319.9 %reduce-scatter.12.cloned.1.call-start = ((), (), s32[]{:S(2)}) async-start(), calls=%async_computation.11 | async-start | bytes 10485760 | tf_op jit(solution)/shard_map/reduce_scatter | solution.py:224
  35.4 159.1 %copy-start.18 = (bf16[256,1024]{1,0:T(8,128)(2,1)}, bf16[256,1024]{1,0:T(8,128)(2,1)S(1)}, u32[]{:S(2)}) copy-start(bf16[256,1024]{1,0:T(8,128)(2,1)S(1)} %all_gather.30) | copy-start | bytes 1572868
  36.5 94.6 %copy-start.10 = (f32[2048,64]{0,1:T(8,128)}, f32[2048,64]{0,1:T(8,128)S(1)}, u32[]{:S(2)}) copy-start(f32[2048,64]{0,1:T(8,128)S(1)} %get-tuple-element.321) | copy-start | bytes 1572868
  200.2 171.1 %all-gather.16.cloned.1.call-start = ((), (), s32[]{:S(2)}) async-start(), calls=%async_computation.14 | async-start | bytes 1511424 | tf_op jit(solution)/shard_map/all_gather | solution.py:205
  202.0 252.1 %all-gather.18.cloned.1.call-start = ((), (), s32[]{:S(2)}) async-start(), calls=%async_computation.16 | async-start | bytes 5242880 | tf_op jit(solution)/shard_map/all_gather | solution.py:246
  205.0 280.7 %all-gather.14.cloned.1.call-start = ((), (), s32[]{:S(2)}) async-start(), calls=%async_computation.13 | async-start | bytes 3022848 | tf_op jit(solution)/shard_map/all_gather | solution.py:204
  205.9 362.2 %all-gather.12.cloned.1.call-start = ((), (), s32[]{:S(2)}) async-start(), calls=%async_computation.12 | async-start | bytes 5242880 | tf_op jit(solution)/shard_map/all_gather | solution.py:231
  347.9 401.9 %reduce-scatter.16.cloned.1.call-start = ((), (), s32[]{:S(2)}) async-start(), calls=%async_computation.17 | async-start | bytes 10485760 | tf_op jit(solution)/shard_map/reduce_scatter | solution.py:254
  606.6 222.9 %reduce-scatter.14.cloned.1.call-start = ((), (), s32[]{:S(2)}) async-start(), calls=%async_computation.15 | async-start | bytes 5242880 | tf_op jit(solution)/shard_map/reduce_scatter | solution.py:239
  614.4 215.1 %copy-start.13 = (bf16[512,1024]{1,0:T(8,128)(2,1)S(1)}, bf16[512,1024]{1,0:T(8,128)(2,1)}, u32[]{:S(2)}) copy-start(bf16[512,1024]{1,0:T(8,128)(2,1)} %param.23) | copy-start | bytes 3145732
  614.4 301.2 %all-gather.20.cloned.1.call-start = ((), (), s32[]{:S(2)}) async-start(), calls=%async_computation.18 | async-start | bytes 5242880 | tf_op jit(solution)/shard_map/all_gather | solution.py:262
  834.2 297.6 %reduce-scatter.26.cloned.1.call-start = ((), (), s32[]{:S(2)}) async-start(), calls=%async_computation.23 | async-start | bytes 3022848 | tf_op jit(solution)/shard_map/reduce_scatter | solution.py:302
  841.8 292.3 %reduce-scatter.24.cloned.1.call-start = ((), (), s32[]{:S(2)}) async-start(), calls=%async_computation.22 | async-start | bytes 6045696 | tf_op jit(solution)/shard_map/reduce_scatter | solution.py:301
  852.8 284.3 %reduce-scatter.22.cloned.1.call-start = ((), (), s32[]{:S(2)}) async-start(), calls=%async_computation.21 | async-start | bytes 1179648 | tf_op jit(solution)/shard_map/reduce_scatter | solution.py:300
  1099.9 85.1 %reduce-scatter.20.cloned.1.call-start = ((), (), s32[]{:S(2)}) async-start(), calls=%async_computation.20 | async-start | bytes 3538944 | tf_op jit(solution)/shard_map/reduce_scatter | solution.py:299
  1124.0 140.0 %reduce-scatter.18.cloned.1.call-start = ((), (), s32[]{:S(2)}) async-start(), calls=%async_computation.19 | async-start | bytes 5242880 | tf_op jit(solution)/shard_map/reduce_scatter | solution.py:286
  1130.5 171.6 %reduce-scatter.28.cloned.1.call-start = ((), (), s32[]{:S(2)}) async-start(), calls=%async_computation.24 | async-start | bytes 589824
  1137.0 126.9 %copy-start.5 = (bf16[512,1024]{1,0:T(8,128)(2,1)S(1)}, bf16[512,1024]{1,0:T(8,128)(2,1)}, u32[]{:S(2)}) copy-start(bf16[512,1024]{1,0:T(8,128)(2,1)} %param.22) | copy-start | bytes 3145732
  1137.0 126.9 %copy-start.30 = (f32[1,1024]{1,0:T(1,128)S(1)}, f32[1,1024]{1,0:T(1,128)}, u32[]{:S(2)}) copy-start(f32[1,1024]{1,0:T(1,128)} %copy-done.29) | copy-start | bytes 12292
  1137.0 126.9 %copy-start.32 = (f32[512]{0:T(512)S(1)}, f32[512]{0:T(512)}, u32[]{:S(2)}) copy-start(f32[512]{0:T(512)} %copy-done.31) | copy-start | bytes 6148
  1137.0 126.9 %copy-start.34 = (f32[512]{0:T(512)S(1)}, f32[512]{0:T(512)}, u32[]{:S(2)}) copy-start(f32[512]{0:T(512)} %copy-done.33) | copy-start | bytes 6148
  1139.0 127.3 %copy-start.35 = (f32[1024]{0:T(1024)S(1)}, f32[1024]{0:T(1024)}, u32[]{:S(2)}) copy-start(f32[1024]{0:T(1024)} %get-tuple-element.212) | copy-start | bytes 12292
  (41 other events, 648.7 us)
Sparse Core Ops, SparseCore 0:
  10.5 29.0 all-gather.9
  41.7 80.9 all-gather.7
  200.3 142.9 reduce-scatter.11
  345.6 25.5 all-gather.15
  373.3 80.7 all-gather.17
  456.4 29.3 all-gather.13
  487.3 80.7 all-gather.11
  606.7 142.9 reduce-scatter.15
  752.1 77.4 reduce-scatter.13
  834.3 81.2 all-gather.19
  919.4 43.1 reduce-scatter.25
  966.3 57.1 reduce-scatter.23
  1100.0 35.0 reduce-scatter.21
  1138.8 46.2 reduce-scatter.19
  1187.2 76.7 reduce-scatter.17
  1267.4 34.6 reduce-scatter.27
where the time goes:
time: 1330 us; the launch traced here: 1320 us
  waiting for transfers between devices  860 us (65%)
  matrix products  202 us (15%)
  other arithmetic  113 us (8%)
  local copies, waits for them, and re-layouts  83.8 us (6%)
  blocking collectives  32.8 us (2%)
  between operations  15.1 us (1%)
  loops' own time  13.5 us (1%)
    reduce_scatter x1, waiting for transfers between devices, body(): lax.psum_scatter(jnp.dot(attended, proj_all, preferred_element_type=jnp.f...  137 us
    reduce_scatter x1, waiting for transfers between devices, body(): lax.psum_scatter(jnp.einsum('krf,kdf->rd', grad_expanded, expand_all, pre...  135 us
    all_gather x1, waiting for transfers between devices, body(): lax.all_gather((normed_one * gain_values[0]).astype(jnp.bfloat16), 'tenso...  83.2 us
    all_gather x1, waiting for transfers between devices, body(): lax.all_gather(grad_masked.astype(jnp.bfloat16), 'tensor', axis=0, tiled=...  82.8 us
    all_gather x1, waiting for transfers between devices, body(): lax.all_gather((normed_two * gain_values[1]).astype(jnp.bfloat16), 'tenso...  82.4 us
    reduce_scatter x1, waiting for transfers between devices, body(): lax.psum_scatter(jnp.dot(hidden, reduce_all, preferred_element_type=jnp.f...  76.2 us
    reduce_scatter x1, waiting for transfers between devices, body(): lax.psum_scatter(jnp.einsum('krc,kdc->rd', grad_projected, qkv_all, prefe...  71.9 us
    all_gather x1, waiting for transfers between devices, body(): lax.all_gather(grad_middle.astype(jnp.bfloat16), 'tensor', axis=0, tiled=...  62.8 us
  transfers between devices with their start and end apart: 16, of which 13 were waited for; matrix products, arithmetic and copies ran while one was open for 21% of the time, Pallas kernels for 0%

commit v1 on v0

v1 whole, which is shorter than its diff:
```python
import jax
import jax.numpy as jnp
from jax import lax
from jax.experimental import pallas as pl
from jax.experimental.pallas import tpu as pltpu
from jax.sharding import PartitionSpec as P

MAXLEN = 512
QBLOCK = 512
STEP = 10
HEAD_DIM = 64


NORM_EPS = 1e-05
ROPE_BASE = 160000.0
NEG_LARGE = -1000000000.0
BETA_ONE = 0.9
BETA_TWO = 0.98
ADAM_EPS = 1e-06
LEARN_RATE = 0.05
GAIN_RATE = 0.2
WEIGHT_DECAY = 0.01


def layout(lengths, count):
    ends = jnp.cumsum(lengths)
    starts = ends - lengths
    row_ids = jnp.arange(count, dtype=jnp.int32)
    member = (row_ids[:, None] >= starts[None, :]) & (row_ids[:, None] < ends[None, :])
    slot_ids = jnp.arange(lengths.shape[0], dtype=jnp.int32)
    valid = jnp.any(member, axis=1)
    segment = jnp.where(valid, jnp.sum(jnp.where(member, slot_ids[None, :], 0), axis=1), -1)
    position = row_ids - jnp.sum(jnp.where(member, starts[None, :], 0), axis=1)
    return (segment, position, valid)


def rotary(values, position):
    head_size = values.shape[-1]
    half_size = head_size // 2
    exponents = jnp.arange(half_size, dtype=jnp.float32) * (2.0 / head_size)
    frequency = ROPE_BASE ** (-exponents)
    angles = position.astype(jnp.float32)[:, None] * frequency[None, :]
    cosine_table = jnp.concatenate([jnp.cos(angles), jnp.cos(angles)], axis=-1)[:, None, :]
    sine_table = jnp.concatenate([jnp.sin(angles), jnp.sin(angles)], axis=-1)[:, None, :]
    rotated = jnp.concatenate([-values[..., half_size:], values[..., :half_size]], axis=-1)
    return values * cosine_table + rotated * sine_table


def normalize(values):
    centered = values - jnp.mean(values, axis=-1, keepdims=True)
    inverse = lax.rsqrt(jnp.mean(centered * centered, axis=-1, keepdims=True) + NORM_EPS)
    return (centered * inverse, inverse)


def norm_back(grad_normed, normed, inverse):
    first_mean = jnp.mean(grad_normed, axis=-1, keepdims=True)
    second_mean = jnp.mean(grad_normed * normed, axis=-1, keepdims=True)
    return inverse * (grad_normed - first_mean - normed * second_mean)


TILE = 256
PAIR = 2 * HEAD_DIM


def matmul_t(left, right):
    return lax.dot_general(left, right, (((1,), (1,)), ((), ())), preferred_element_type=jnp.float32)


def matmul_n(left, right):
    return lax.dot_general(left, right, (((1,), (0,)), ((), ())), preferred_element_type=jnp.float32)


def matmul_tn(left, right):
    return lax.dot_general(left, right, (((0,), (0,)), ((), ())), preferred_element_type=jnp.float32)


def head_lanes(rows):
    return lax.broadcasted_iota(jnp.int32, (rows, PAIR), 1) // HEAD_DIM


def forward_kernel(seg_q, seg_k, queries, keys, values, mixed, log_totals):
    key_block = keys[...]
    value_block = values[...]
    lanes = head_lanes(TILE)
    for tile in range(queries.shape[0] // TILE):
        rows = pl.ds(tile * TILE, TILE)
        seen = seg_q[rows, :] == seg_k[...]
        query_pair = queries[rows, :]
        parts = []
        for head in range(2):
            query = jnp.where(lanes == head, query_pair, jnp.zeros_like(query_pair))
            scores = jnp.where(seen, matmul_t(query, key_block), NEG_LARGE)
            top = jnp.max(scores, axis=-1, keepdims=True)
            raw = jnp.exp(scores - top)
            total = jnp.sum(raw, axis=-1, keepdims=True)
            weights = (raw * (1.0 / total)).astype(jnp.bfloat16)
            parts.append(matmul_n(weights, value_block))
            log_totals[head, rows, :] = top + jnp.log(total)
        mixed[rows, :] = jnp.where(lanes == 0, parts[0], parts[1]).astype(jnp.bfloat16)


def backward_kernel(seg_q, seg_k, queries, keys, values, grad_mixed, log_totals, grad_q, grad_k, grad_v):
    key_block = keys[...]
    value_block = values[...]
    lanes = head_lanes(TILE)
    for tile in range(queries.shape[0] // TILE):
        rows = pl.ds(tile * TILE, TILE)
        seen = seg_q[rows, :] == seg_k[...]
        query_pair = queries[rows, :]
        grad_pair = grad_mixed[rows, :]
        parts = []
        for head in range(2):
            query = jnp.where(lanes == head, query_pair, jnp.zeros_like(query_pair))
            grad = jnp.where(lanes == head, grad_pair, jnp.zeros_like(grad_pair))
            scores = jnp.where(seen, matmul_t(query, key_block), NEG_LARGE)
            probs = jnp.exp(scores - log_totals[head, rows, :])
            grad_probs = matmul_t(grad, value_block)
            inner = jnp.sum(probs * grad_probs, axis=-1, keepdims=True)
            grad_scores = (probs * (grad_probs - inner)).astype(jnp.bfloat16)
            parts.append(matmul_n(grad_scores, key_block))
            key_part = matmul_tn(grad_scores, query)
            value_part = matmul_tn(probs.astype(jnp.bfloat16), grad)
            if tile == 0 and head == 0:
                grad_k[...] = key_part
                grad_v[...] = value_part
            else:
                grad_k[...] += key_part
                grad_v[...] += value_part
        grad_q[rows, :] = jnp.where(lanes == 0, parts[0], parts[1]) * (HEAD_DIM**-0.5)


def attention_specs(rows, window):
    whole_q = pl.BlockSpec((rows, 1), lambda pair: (0, 0))
    whole_k = pl.BlockSpec((1, window), lambda pair: (0, 0))
    by_rows = pl.BlockSpec((rows, PAIR), lambda pair: (0, pair))
    by_window = pl.BlockSpec((window, PAIR), lambda pair: (0, pair))
    totals = pl.BlockSpec((2, rows, 1), lambda pair: (pair, 0, 0))
    return whole_q, whole_k, by_rows, by_window, totals


def attend_forward(seg_q, seg_k, queries, keys, values):
    rows, width = queries.shape
    window = keys.shape[0]
    whole_q, whole_k, by_rows, by_window, totals = attention_specs(rows, window)
    return pl.pallas_call(
        forward_kernel,
        grid=(width // PAIR,),
        in_specs=[whole_q, whole_k, by_rows, by_window, by_window],
        out_specs=[by_rows, totals],
        out_shape=[
            jax.ShapeDtypeStruct((rows, width), jnp.bfloat16),
            jax.ShapeDtypeStruct((width // HEAD_DIM, rows, 1), jnp.float32),
        ],
        compiler_params=pltpu.CompilerParams(vmem_limit_bytes=48 * 1024 * 1024),
        cost_estimate=pl.CostEstimate(
            flops=4 * rows * window * width, bytes_accessed=8 * window * width, transcendentals=rows * window * 16
        ),
        name="attend_forward",
    )(seg_q, seg_k, queries, keys, values)


def attend_backward(seg_q, seg_k, queries, keys, values, grad_mixed, log_totals):
    rows, width = queries.shape
    window = keys.shape[0]
    whole_q, whole_k, by_rows, by_window, totals = attention_specs(rows, window)
    return pl.pallas_call(
        backward_kernel,
        grid=(width // PAIR,),
        in_specs=[whole_q, whole_k, by_rows, by_window, by_window, by_rows, totals],
        out_specs=[by_rows, by_window, by_window],
        out_shape=[
            jax.ShapeDtypeStruct((rows, width), jnp.float32),
            jax.ShapeDtypeStruct((window, width), jnp.float32),
            jax.ShapeDtypeStruct((window, width), jnp.float32),
        ],
        compiler_params=pltpu.CompilerParams(vmem_limit_bytes=48 * 1024 * 1024),
        cost_estimate=pl.CostEstimate(
            flops=10 * rows * window * width, bytes_accessed=16 * window * width, transcendentals=rows * window * 16
        ),
        name="attend_backward",
    )(seg_q, seg_k, queries, keys, values, grad_mixed, log_totals)


def halve(blocks, axis, name, bit):
    mine = (lax.axis_index(name) >> bit) & 1
    keep = lax.dynamic_index_in_dim(blocks, mine, axis, keepdims=False)
    send = lax.dynamic_index_in_dim(blocks, 1 - mine, axis, keepdims=False)
    pairs = [(i, i ^ (1 << bit)) for i in range(lax.axis_size(name))]
    return keep.astype(jnp.float32) + lax.ppermute(send, name, pairs).astype(jnp.float32)


def dp_halves(grads, axis, turned):
    bits = (lax.axis_size("dp") - 1).bit_length()
    shape = grads.shape
    blocks = grads.reshape(*shape[:axis], *[2] * bits, shape[axis] >> bits, *shape[axis + 1 :])
    left = list(range(bits - 1, -1, -1))
    order = [0] + (list(range(bits - 1, 0, -1)) if turned else list(range(1, bits)))
    for bit in order:
        place = left.index(bit)
        blocks = halve(blocks, axis + place, "dp", bit).astype(jnp.bfloat16)
        left.pop(place)
    return blocks


def tensor_halves(blocks):
    bits = (lax.axis_size("tensor") - 1).bit_length()
    blocks = blocks.reshape(*[2] * bits, *blocks.shape[1:])
    for bit in range(bits):
        blocks = halve(blocks.astype(jnp.bfloat16), bits - 1 - bit, "tensor", bit)
    return blocks


def adam_step(param, grad, moment, square, rate, decay):
    moment = BETA_ONE * moment + (1.0 - BETA_ONE) * grad
    square = BETA_TWO * square + (1.0 - BETA_TWO) * grad * grad
    moment_hat = moment / (1.0 - BETA_ONE**STEP)
    square_hat = square / (1.0 - BETA_TWO**STEP)
    updated = param - rate * (moment_hat / (jnp.sqrt(square_hat) + ADAM_EPS) + decay * param)
    return (moment, square, updated)


def gated(pre_part, gate_part):
    return jax.nn.gelu(pre_part, approximate=False) * gate_part


def body(
    inputs,
    cotangent,
    seq_lens,
    gains,
    w_qkv,
    w_out,
    w_in,
    w_down,
    moment_gains,
    square_gains,
    moment_qkv,
    square_qkv,
    moment_out,
    square_out,
    moment_in,
    square_in,
    moment_down,
    square_down,
):
    both = ("dp", "tensor")
    dp_size, tp_size = lax.axis_size("dp"), lax.axis_size("tensor")
    local_rows, width = inputs.shape
    heads = width // HEAD_DIM
    group_rows = local_rows * tp_size
    my_index = lax.axis_index("tensor")
    my_start = my_index * local_rows
    half = jnp.bfloat16
    upward = [(i, i + 1) for i in range(tp_size - 1)]
    downward = [(i + 1, i) for i in range(tp_size - 1)]

    depth, qkv_cols = w_qkv.shape[1], w_qkv.shape[2]
    first_rows_count = 4 * depth
    gain_cols = gains.shape[1]
    gain_row = jnp.pad(gains.astype(half).reshape(1, 2 * gain_cols), ((0, 15), (0, qkv_cols - 2 * gain_cols)))
    first_pack = jnp.concatenate(
        [w_qkv.astype(half).reshape(3 * depth, qkv_cols), w_out.astype(half).T, gain_row]
    )
    units = w_in.shape[2]
    second_pack = jnp.concatenate([w_in.astype(half).transpose(0, 2, 1), w_down.astype(half)[None]])
    first_all = lax.all_gather(first_pack, both, axis=0)
    second_all = lax.all_gather(second_pack, both, axis=0)

    first_all = first_all.reshape(dp_size, tp_size, first_rows_count + 16, qkv_cols)
    gain_values = (
        first_all[:, 0, first_rows_count, : 2 * gain_cols]
        .reshape(dp_size, 2, gain_cols).transpose(1, 0, 2).reshape(2, width)
    ).astype(jnp.float32)
    first_full = (
        first_all[:, :, :first_rows_count].reshape(dp_size, tp_size, 4, depth, qkv_cols)
        .transpose(2, 0, 3, 1, 4).reshape(4, width, width)
    )
    qkv_full, out_full = first_full[:3], first_full[3]
    second_full = (
        second_all.reshape(dp_size, tp_size, 3, units, depth).transpose(1, 2, 3, 0, 4)
        .reshape(tp_size, 3, units, width)
    )
    in_full, down_full = second_full[:, :2], second_full[:, 2]

    segment, position, valid = layout(seq_lens[0], group_rows)
    my_valid = lax.dynamic_slice_in_dim(valid, my_start, local_rows, 0).astype(jnp.float32)
    segment = jnp.where(valid, segment, -2 - jnp.arange(group_rows, dtype=jnp.int32))
    pad_segment = jnp.pad(segment, (MAXLEN, MAXLEN), constant_values=-1)
    pad_position = jnp.pad(position, (MAXLEN, MAXLEN))
    window = local_rows + 2 * MAXLEN
    seg_k = lax.dynamic_slice_in_dim(pad_segment, my_start, window, 0)
    pos_k = lax.dynamic_slice_in_dim(pad_position, my_start, window, 0)
    seg_q = seg_k[MAXLEN : MAXLEN + local_rows]
    mine = slice(MAXLEN, MAXLEN + local_rows)

    before = lax.ppermute(inputs[local_rows - MAXLEN :], "tensor", upward)
    after = lax.ppermute(inputs[:MAXLEN], "tensor", downward)
    wide = jnp.concatenate([before, inputs, after]).astype(jnp.float32)
    residual = inputs.astype(jnp.float32)
    normed_wide, inverse_wide = normalize(wide)
    first_rows = (normed_wide * gain_values[0]).astype(half)
    normed_one, inverse_one = normed_wide[mine], inverse_wide[mine]

    def project(rows, weight):
        return jnp.dot(rows, weight, preferred_element_type=jnp.float32)

    def turn(values):
        return rotary(values.reshape(window, heads, HEAD_DIM), pos_k).reshape(window, width)

    def turn_own(values):
        return rotary(values.reshape(local_rows, heads, HEAD_DIM), pos_k[mine]).reshape(local_rows, width)

    query_raw = project(first_rows[mine], qkv_full[0])
    key_raw = project(first_rows, qkv_full[1])
    queries = turn_own(query_raw).astype(half) * half(HEAD_DIM**-0.5)
    keys = turn(key_raw).astype(half)
    values = project(first_rows, qkv_full[2]).astype(half)
    seg_q, seg_k = seg_q[:, None], seg_k[None, :]
    attended, log_totals = attend_forward(seg_q, seg_k, queries, keys, values)
    middle = residual + jnp.einsum("rc,dc->rd", attended, out_full, preferred_element_type=jnp.float32)
    normed_two, inverse_two = normalize(middle)
    second_rows = (normed_two * gain_values[1]).astype(half)
    expanded = jnp.einsum("rd,tkfd->tkrf", second_rows, in_full, preferred_element_type=jnp.float32)
    hidden_full, gated_back = jax.vjp(gated, expanded[:, 0], expanded[:, 1])
    hidden = hidden_full.astype(half)
    outputs = middle + jnp.einsum("trf,tfd->rd", hidden, down_full, preferred_element_type=jnp.float32)

    grad_masked = cotangent.astype(jnp.float32) * my_valid[:, None]
    grad_rows = grad_masked.astype(half)

    def second_share(grads, turn_y):
        blocks = dp_halves(grads.astype(half), 1, turn_y)
        return tensor_halves(blocks)

    grad_down = jnp.einsum("rd,trf->tdf", grad_rows, hidden, preferred_element_type=jnp.float32)
    down_sum = second_share(grad_down, False).T
    grad_hidden = jnp.einsum("rd,tfd->trf", grad_rows, down_full, preferred_element_type=jnp.float32)
    grad_pre, grad_gate = gated_back(grad_hidden)
    grad_expanded = jnp.stack([grad_pre, grad_gate], axis=1).astype(half)
    grad_in_first = jnp.einsum("rd,trf->tdf", second_rows, grad_pre.astype(half), preferred_element_type=jnp.float32)
    grad_in_second = jnp.einsum("rd,trf->tdf", second_rows, grad_gate.astype(half), preferred_element_type=jnp.float32)
    in_sum = jnp.stack([second_share(grad_in_first, True), second_share(grad_in_second, False)])
    grad_second = jnp.einsum("tkrf,tkfd->rd", grad_expanded, in_full, preferred_element_type=jnp.float32)
    gain_two = jnp.sum(grad_second * normed_two, axis=0)
    grad_middle = grad_masked + norm_back(grad_second * gain_values[1], normed_two, inverse_two)
    middle_rows = grad_middle.astype(half)
    grad_out = jnp.einsum("rd,rc->dc", middle_rows, attended, preferred_element_type=jnp.float32).astype(half)
    grad_attended = jnp.einsum("rd,dc->rc", middle_rows, out_full, preferred_element_type=jnp.float32).astype(half)
    grad_q, grad_k, grad_v = attend_backward(seg_q, seg_k, queries, keys, values, grad_attended, log_totals)
    unused, turn_back = jax.vjp(turn, key_raw)
    unused, turn_own_back = jax.vjp(turn_own, query_raw)
    grad_q = turn_own_back(grad_q)[0].astype(half)
    grad_k = turn_back(grad_k)[0].astype(half)
    grad_v = grad_v.astype(half)

    def back(grads, weight):
        return jnp.einsum("rc,dc->rd", grads, weight, preferred_element_type=jnp.float32)

    grad_wide = back(grad_k, qkv_full[1]) + back(grad_v, qkv_full[2])
    grad_own = grad_wide[mine] + back(grad_q, qkv_full[0])
    from_above = lax.ppermute(grad_wide[:MAXLEN].astype(half), "tensor", downward)
    from_below = lax.ppermute(grad_wide[MAXLEN + local_rows :].astype(half), "tensor", upward)
    gain_one = (
        jnp.sum(grad_own * normed_one, axis=0)
        + jnp.sum(grad_wide[:MAXLEN] * normed_wide[:MAXLEN], axis=0)
        + jnp.sum(grad_wide[MAXLEN + local_rows :] * normed_wide[MAXLEN + local_rows :], axis=0)
    )

    def outer(rows, grads):
        return jnp.einsum("rd,rc->dc", rows, grads, preferred_element_type=jnp.float32).astype(half)

    gain_blocks = jnp.stack([gain_one, gain_two]).reshape(2, dp_size, gain_cols).transpose(1, 0, 2)
    gain_blocks = jnp.pad(
        gain_blocks.astype(half).reshape(dp_size, 1, 1, 2 * gain_cols),
        ((0, 0), (0, 15), (0, 0), (0, qkv_cols - 2 * gain_cols)),
    )
    gain_blocks = jnp.broadcast_to(gain_blocks, (dp_size, 16, tp_size, qkv_cols)).reshape(dp_size, 16, width)

    def rows_of(grads):
        return grads.reshape(dp_size, depth, width)

    def first_share(parts, turn_y):
        packed = jnp.concatenate(parts, axis=1)
        count = packed.shape[1]
        block = dp_halves(packed.reshape(dp_size * count, width), 0, turn_y)
        return tensor_halves(block.reshape(count, tp_size, qkv_cols).transpose(1, 0, 2))

    value_out = first_share(
        [rows_of(outer(first_rows, grad_v)), rows_of(grad_out)], False
    )
    query_key = first_share(
        [rows_of(outer(first_rows[mine], grad_q)), rows_of(outer(first_rows, grad_k)), gain_blocks], True
    )
    qkv_sum = jnp.concatenate([query_key[: 2 * depth], value_out[:depth]]).reshape(w_qkv.shape)
    out_sum = value_out[depth:].T
    gain_grads = query_key[2 * depth, : 2 * gain_cols].reshape(2, gain_cols)

    shift_low = jnp.pad(from_below.astype(jnp.float32), ((0, local_rows - MAXLEN), (0, 0)))
    shift_high = jnp.pad(from_above.astype(jnp.float32), ((local_rows - MAXLEN, 0), (0, 0)))
    grad_first = grad_own + shift_low + shift_high
    grad_inputs = grad_middle + norm_back(grad_first * gain_values[0], normed_one, inverse_one)
    gains_new = adam_step(gains, gain_grads, moment_gains, square_gains, GAIN_RATE, 0.0)
    qkv_new = adam_step(w_qkv, qkv_sum, moment_qkv, square_qkv, LEARN_RATE, WEIGHT_DECAY)
    out_new = adam_step(w_out, out_sum, moment_out, square_out, LEARN_RATE, WEIGHT_DECAY)
    in_new = adam_step(w_in, in_sum, moment_in, square_in, LEARN_RATE, WEIGHT_DECAY)
    down_new = adam_step(w_down, down_sum, moment_down, square_down, LEARN_RATE, WEIGHT_DECAY)
    return (
        outputs,
        grad_inputs,
        gains_new[0],
        gains_new[1],
        gains_new[2],
        qkv_new[0],
        qkv_new[1],
        qkv_new[2],
        out_new[0],
        out_new[1],
        out_new[2],
        in_new[0],
        in_new[1],
        in_new[2],
        down_new[0],
        down_new[1],
        down_new[2],
    )


def solution(mesh):
    in_specs = (
        P(("dp", "tensor"), None),
        P(("dp", "tensor"), None),
        P("dp", None),
        P(None, "dp"),
        P(None, "dp", "tensor"),
        P("tensor", "dp"),
        P(None, "dp", "tensor"),
        P("tensor", "dp"),
        P(None, "dp"),
        P(None, "dp"),
        P(None, "dp", "tensor"),
        P(None, "dp", "tensor"),
        P("tensor", "dp"),
        P("tensor", "dp"),
        P(None, "dp", "tensor"),
        P(None, "dp", "tensor"),
        P("tensor", "dp"),
        P("tensor", "dp"),
    )
    out_specs = (
        P(("dp", "tensor"), None),
        P(("dp", "tensor"), None),
        P(None, "dp"),
        P(None, "dp"),
        P(None, "dp"),
        P(None, "dp", "tensor"),
        P(None, "dp", "tensor"),
        P(None, "dp", "tensor"),
        P("tensor", "dp"),
        P("tensor", "dp"),
        P("tensor", "dp"),
        P(None, "dp", "tensor"),
        P(None, "dp", "tensor"),
        P(None, "dp", "tensor"),
        P("tensor", "dp"),
        P("tensor", "dp"),
        P("tensor", "dp"),
    )
    return jax.shard_map(body, mesh=mesh, in_specs=in_specs, out_specs=out_specs, check_vma=False)
```

time: 1330 us -> 743 us (0.56)
  waiting for transfers between devices: 860 us -> 171 us
  local copies, waits for them, and re-layouts: 83.8 us -> 227 us
  Pallas kernels: 0 us -> 81.1 us
  matrix products: 202 us -> 122 us
  blocking collectives: 32.8 us -> 0 us
  starting transfers between devices: 1.54 us -> 31.5 us
  other arithmetic: 113 us -> 88.9 us
  loops' own time: 13.5 us -> 0 us
    reduce_scatter x8 -> x0, waiting for transfers between devices: 467 us -> none  [the longest x1 137 us: body(): lax.psum_scatter(jnp.dot(attended, proj_all, preferred_element_type=jnp.f...]
    all_gather x7 -> x2, waiting for transfers between devices: 361 us -> 42 us  [the longest x1 34.6 us: body(): first_all = lax.all_gather(first_pack, both, axis=0)]
    ppermute x0 -> x29, waiting for transfers between devices: none -> 129 us  [the longest x25 81.5 us: halve(): lax.ppermute(send, name, pairs).astype(jnp.float32)]
    pallas_call x0 -> x2, Pallas kernels: none -> 81.1 us  [the longest x1 48 us: attend_backward(): pl.pallas_call(backward_kernel, grid=(width // PAIR,), in_specs=[whole_q,...]
    dot_general x40 -> x19, matrix products: 202 us -> 122 us  [the longest x3 23.5 us: back(): jnp.einsum('rc,dc->rd', grads, weight, preferred_element_type=jnp.float32)]
    reshape x2 -> x7, local copies, waits for them, and re-layouts: 3.13 us -> 83.3 us  [the longest x3 39 us: dp_halves(): grads.reshape(*shape[:axis], *[2] * bits, shape[axis] >> bits, *shape[axi...]
    dynamic_update_slice x8 -> x0, local copies, waits for them, and re-layouts: 46.5 us -> none  [attend_backward(): lax.scan(one_block, (zeros, zeros), jnp.arange(total // block, dtype=jnp....]
    dynamic_slice x24 -> x5, local copies, waits for them, and re-layouts: 6.25 us -> 41.2 us  [the longest x4 41.1 us: halve(): keep = lax.dynamic_index_in_dim(blocks, mine, axis, keepdims=False)]
  transfers between devices with their start and end apart: 16 -> 31, of which waited for: 13 -> 15; matrix products, arithmetic and copies ran while one was open for 21% -> 34% of each run, Pallas kernels for 0% -> 4%
where the time goes in v1:
time: 743 us; the launch traced here: 737 us
  local copies, waits for them, and re-layouts  227 us (31%)
  waiting for transfers between devices  171 us (23%)
  matrix products  122 us (16%)
  other arithmetic  88.9 us (12%)
  Pallas kernels  81.1 us (11%)
  starting transfers between devices  31.5 us (4%)
  between operations  15.6 us (2%)
    ppermute x25, waiting for transfers between devices, halve(): lax.ppermute(send, name, pairs).astype(jnp.float32)  81.5 us
    pallas_call x1, Pallas kernels, attend_backward(): pl.pallas_call(backward_kernel, grid=(width // PAIR,), in_specs=[whole_q,...  48 us
    dynamic_slice x4, local copies, waits for them, and re-layouts, halve(): keep = lax.dynamic_index_in_dim(blocks, mine, axis, keepdims=False)  41.1 us
    reshape x3, local copies, waits for them, and re-layouts, dp_halves(): grads.reshape(*shape[:axis], *[2] * bits, shape[axis] >> bits, *shape[axi...  39 us
    all_gather x1, waiting for transfers between devices, body(): first_all = lax.all_gather(first_pack, both, axis=0)  34.6 us
    pallas_call x1, Pallas kernels, attend_forward(): pl.pallas_call(forward_kernel, grid=(width // PAIR,), in_specs=[whole_q,...  33.1 us
    unnamed x179, local copies, waits for them, and re-layouts  31.8 us
    reshape x1, local copies, waits for them, and re-layouts, body(): second_full = second_all.reshape(dp_size, tp_size, 3, units, depth).trans...  24.7 us
  transfers between devices with their start and end apart: 31, of which 15 were waited for; matrix products, arithmetic and copies ran while one was open for 34% of the time, Pallas kernels for 4%

profile of v1, /device:TPU:0, one launch (start us, length us, event | category | flops | bytes accessed | tf_op | source)
XLA Modules:
  0.0 737.0 jit_solution(6888363276452681839)
XLA Ops:
  29.0 22.6 %collective-permute-done = bf16[512,1024]{1,0:T(8,128)(2,1)S(1)} collective-permute-done((bf16[512,1024]{1,0:T(8,128)(2,1)S(1)}, bf16[512,1024]{1,0:T(8,128)(2,1)S(1)}, u32[]{:S(2)}, u32[]{:S(2)}) %collective-permute-start) | collective-permute-done | bytes 1048608 | tf_op jit(solution)/shard_map/ppermute | solution.py:296
  65.0 34.6 %all-gather.5.cloned.1.call-done = bf16[16896,256]{1,0:T(8,128)(2,1)} async-done(((bf16[528,256]{1,0:T(8,128)(2,1)}), bf16[16896,256]{1,0:T(8,128)(2,1)}) %all-gather.5.cloned.1.call-update) | async-done | bytes 8650768 | tf_op jit(solution)/shard_map/all_gather | solution.py:266
  162.2 9.0 %convolution_convert_fusion.values = bf16[1536,1024]{1,0:T(8,128)(2,1)} fusion(bf16[1536,1024]{1,0:T(8,128)(2,1)} %copy-done.34, bf16[128,8,8,128]{3,2,1,0:T(8,128)(2,1)} %bitcast.504), kind=kOutput, calls=%fused_computation.74 | convolution fusion | flops 3222798336 | bytes 8388608 | tf_op jit(solution)/shard_map/dot_general | solution.py:305
  171.3 33.1 %attend_forward.1 = (bf16[512,1024]{1,0:T(8,128)(2,1)S(1)}, f32[16,512,1]{2,1,0:T(8,128)}) custom-call(s32[512,1]{1,0:T(8,128)S(1)} %copy.200.seg_q, s32[1,1536]{1,0:T(1,128)S(1)} %broadcast_in_dim.34.seg_k, bf16[512,1024]{1,0:T(8,128)(2,1)S(1)} %copy-done.1, bf16[1536,1024]{1,0:T(8,128)(2,1)S(1)} %copy.202.keys, ...), custom_call_target="tpu_custom_call" | custom-call | flops 3221225472 | bytes 12582912 | tf_op jit(solution)/shard_map/attend_forward/pallas_call | solution.py:145
  213.5 19.0 %copy.301 = bf16[8,4,3,656,128]{4,0,3,2,1:T(8,128)(2,1)} copy(bf16[8,4,3,656,128]{4,3,2,1,0:T(8,128)(2,1)} %bitcast.479) | data formatting | bytes 32243712 | tf_op jit(solution)/shard_map/reshape | solution.py:280
  232.5 24.7 %reshape.321 = bf16[4,3,656,1024]{3,2,1,0:T(8,128)(2,1)} reshape(bf16[4,3,656,8,128]{4,3,2,1,0:T(8,128)(2,1)} %bitcast.467) | data formatting | bytes 32243712 | tf_op jit(solution)/shard_map/reshape | solution.py:281
  257.2 9.0 %convolution_bitcast_fusion = f32[4,2,512,656]{2,3,1,0:T(8,128)S(1)} fusion(bf16[4,3,656,1024]{3,2,1,0:T(8,128)(2,1)} %reshape.321, f32[512,1024]{1,0:T(8,128)S(1)} %get-tuple-element.171, f32[1024]{0:T(1024)S(1)} %bitcast.520, f32[512]{0:T(512)S(1)} %add_rsqrt_fusion.1, f32[512]{0:T(512)S(1)} %broadcast_multiply_fusion.7), kind=kOutput, calls=%fused_computation.73 | convolution fusion | flops 5505024000 | bytes 28975104 | tf_op jit(solution)/shard_map/rd,tkfd->tkrf/dot_general | solution.py:323
  266.2 16.9 %fusion.21 = (bf16[4,512,656]{1,2,0:T(8,128)(2,1)S(1)}, f32[4,512,656]{1,2,0:T(8,128)S(1)}, f32[4,656,512]{2,1,0:T(8,128)S(1)}) fusion(f32[4,2,512,656]{2,3,1,0:T(8,128)S(1)} %convolution_bitcast_fusion, bf16[512,1024]{1,0:T(8,128)(2,1)S(1)} %copy-done.52, f32[512]{0:T(512)S(1)} %copy-done.70, bf16[4,3,656,1024]{3,2,1,0:T(8,128)(2,1)} %reshape.321), kind=kOutput, calls=%fused_computation.42 | convolution fusion | flops 2851110912 | bytes 30607360 | tf_op jit(solution)/shard_map/rd,tfd->trf/dot_general | solution.py:337
  299.9 10.4 %fusion.60 = (bf16[1024]{0:T(1024)(128)(2,1)S(1)}, f32[512]{0:T(512)S(1)}, f32[512]{0:T(512)S(1)}, f32[512,1024,1,1]{1,0,3,2:T(8,128)S(1)}) fusion(f32[512,1024]{1,0:T(8,128)S(1)} %get-tuple-element.171, f32[512]{0:T(512)S(1)} %add_rsqrt_fusion.1, f32[512]{0:T(512)S(1)} %broadcast_multiply_fusion.7, f32[1024]{0:T(1024)S(1)} %bitcast.523, ...), kind=kOutput, calls=%fused_computation.120 | convolution fusion | flops 5509806080 | bytes 20330496 | tf_op jit(solution)/shard_map/tkrf,tkfd->rd/dot_general | solution.py:343
  315.5 48.0 %attend_backward.1 = (f32[512,1024]{1,0:T(8,128)S(1)}, f32[1536,1024]{1,0:T(8,128)}, f32[1536,1024]{1,0:T(8,128)}) custom-call(s32[512,1]{1,0:T(8,128)S(1)} %copy.200.seg_q, s32[1,1536]{1,0:T(1,128)S(1)} %broadcast_in_dim.34.seg_k, bf16[512,1024]{1,0:T(8,128)(2,1)S(1)} %copy-done.2, bf16[1536,1024]{1,0:T(8,128)(2,1)} %copy-done, ...), custom_call_target="tpu_custom_call" | custom-call | flops 8053063680 | bytes 25165824 | tf_op jit(solution)/shard_map/attend_backward/pallas_call | solution.py:166
  385.1 8.9 %fusion.114 = f32[1536,1024]{1,0:T(8,128)} fusion(bf16[1536,1024]{0,1:T(8,128)(2,1)} %bitcast.490, bf16[128,8,8,128]{3,2,1,0:T(8,128)(2,1)} %bitcast.484), kind=kOutput, calls=%fused_computation.291 | convolution fusion | flops 3221225472 | bytes 11534336 | tf_op jit(solution)/shard_map/rc,dc->rd/dot_general | solution.py:357
  403.7 13.0 %reshape.334 = bf16[4,2,2,2,128,656]{4,3,2,1,5,0:T(2,128)(2,1)} reshape(bf16[4,1024,656]{1,2,0:T(8,128)(2,1)} %convert_bitcast_fusion) | data formatting | bytes 10747904 | tf_op jit(solution)/shard_map/reshape | solution.py:195
  416.7 13.8 %constant_dynamic-slice_fusion.1 = (bf16[4,2,2,1,128,656]{4,3,2,1,5,0:T(2,128)(2,1)}, bf16[4,2,2,1,128,656]{4,3,2,1,5,0:T(2,128)(2,1)S(1)}) fusion(bf16[4,2,2,2,128,656]{4,3,2,1,5,0:T(2,128)(2,1)} %reshape.334, s32[]{:T(128)S(6)} %select_n.114, s32[]{:T(128)S(6)} %select_n.115), kind=kLoop, calls=%fused_computation.257 | loop fusion | bytes 10747912 | tf_op jit(solution)/shard_map/jit(dynamic_index_in_dim)/dynamic_slice | solution.py:186
  432.8 13.0 %reshape.330 = bf16[4,2,2,2,128,656]{4,3,2,1,5,0:T(2,128)(2,1)} reshape(bf16[4,1024,656]{1,2,0:T(8,128)(2,1)} %convert_bitcast_fusion.2) | data formatting | bytes 10747904 | tf_op jit(solution)/shard_map/reshape | solution.py:195
  445.8 13.6 %constant_dynamic-slice_fusion.5 = (bf16[4,2,2,1,128,656]{4,3,2,1,5,0:T(2,128)(2,1)}, bf16[4,2,2,1,128,656]{4,3,2,1,5,0:T(2,128)(2,1)S(1)}) fusion(bf16[4,2,2,2,128,656]{4,3,2,1,5,0:T(2,128)(2,1)} %reshape.330, s32[]{:T(128)S(6)} %select_n.114, s32[]{:T(128)S(6)} %select_n.115), kind=kLoop, calls=%fused_computation.261 | loop fusion | bytes 10747912 | tf_op jit(solution)/shard_map/jit(dynamic_index_in_dim)/dynamic_slice | solution.py:186
  461.6 13.0 %reshape.332 = bf16[4,2,2,2,128,656]{4,3,2,1,5,0:T(2,128)(2,1)} reshape(bf16[4,1024,656]{1,2,0:T(8,128)(2,1)} %convert_bitcast_fusion.1) | data formatting | bytes 10747904 | tf_op jit(solution)/shard_map/reshape | solution.py:195
  474.7 13.6 %constant_dynamic-slice_fusion.3 = (bf16[4,2,2,1,128,656]{4,3,2,1,5,0:T(2,128)(2,1)}, bf16[4,2,2,1,128,656]{4,3,2,1,5,0:T(2,128)(2,1)S(1)}) fusion(bf16[4,2,2,2,128,656]{4,3,2,1,5,0:T(2,128)(2,1)} %reshape.332, s32[]{:T(128)S(6)} %select_n.114, s32[]{:T(128)S(6)} %select_n.115), kind=kLoop, calls=%fused_computation.259 | loop fusion | bytes 10747912 | tf_op jit(solution)/shard_map/jit(dynamic_index_in_dim)/dynamic_slice | solution.py:186
  494.5 8.6 %convolution_convert_fusion.2 = bf16[1024,1024]{1,0:T(8,128)(2,1)} fusion(bf16[1536,1024]{1,0:T(8,128)(2,1)} %copy-done.34, f32[1536,1024]{1,0:T(8,128)} %get-tuple-element.25), kind=kOutput, calls=%fused_computation.138 | convolution fusion | flops 3223846912 | bytes 11534336 | tf_op jit(solution)/shard_map/rd,rc->dc/dot_general | solution.py:370
  517.3 9.0 %convolution_add_fusion = f32[1536,1024]{1,0:T(8,128)S(1)} fusion(f32[1536,1024]{1,0:T(8,128)} %fusion.114, bf16[128,8,8,128]{3,2,1,0:T(8,128)(2,1)S(1)} %bitcast.505, f32[1536,1024]{1,0:T(8,128)} %get-tuple-element.25), kind=kOutput, calls=%fused_computation.70 | convolution fusion | flops 3224371200 | bytes 20971520 | tf_op jit(solution)/shard_map/rc,dc->rd/dot_general | solution.py:357
  539.6 12.4 %collective-permute-done.2 = bf16[512,1024]{1,0:T(8,128)(2,1)S(1)} collective-permute-done((bf16[512,1024]{1,0:T(8,128)(2,1)S(1)}, bf16[512,1024]{1,0:T(8,128)(2,1)S(1)}, u32[]{:S(2)}, u32[]{:S(2)}) %collective-permute-start.2) | collective-permute-done | bytes 1048608 | tf_op jit(solution)/shard_map/ppermute | solution.py:362
  586.6 15.1 %collective-permute-done.10 = bf16[2,256,1024]{1,2,0:T(8,128)(2,1)S(1)} collective-permute-done((bf16[2,256,1024]{1,2,0:T(8,128)(2,1)S(1)}, bf16[2,256,1024]{1,2,0:T(8,128)(2,1)S(1)}, u32[]{:S(2)}, u32[]{:S(2)}) %collective-permute-start.10) | collective-permute-done | bytes 1048608 | tf_op jit(solution)/shard_map/ppermute | solution.py:189
  609.2 17.4 %collective-permute-done.11 = bf16[256,1024]{0,1:T(8,128)(2,1)S(1)} collective-permute-done((bf16[256,1024]{0,1:T(8,128)(2,1)S(1)}, bf16[256,1024]{0,1:T(8,128)(2,1)S(1)}, u32[]{:S(2)}, u32[]{:S(2)}) %collective-permute-start.11) | collective-permute-done | bytes 524320 | tf_op jit(solution)/shard_map/ppermute | solution.py:189
  646.3 13.1 %collective-permute-done.20 = bf16[4,2,128,656]{2,3,1,0:T(8,128)(2,1)} collective-permute-done((bf16[4,2,128,656]{2,3,1,0:T(8,128)(2,1)}, bf16[4,2,128,656]{2,3,1,0:T(8,128)(2,1)}, u32[]{:S(2)}, u32[]{:S(2)}) %collective-permute-start.20) | collective-permute-done | bytes 1343520 | tf_op jit(solution)/shard_map/ppermute | solution.py:189
  699.0 10.4 %collective-permute-done.22 = bf16[2,128,656]{1,2,0:T(8,128)(2,1)} collective-permute-done((bf16[2,128,656]{1,2,0:T(8,128)(2,1)}, bf16[2,128,656]{1,2,0:T(8,128)(2,1)}, u32[]{:S(2)}, u32[]{:S(2)}) %collective-permute-start.22) | collective-permute-done | bytes 335904 | tf_op jit(solution)/shard_map/ppermute | solution.py:189
  (387 shorter events, 319.1 us)
Async XLA Ops:
  7.2 92.4 %all-gather.5.cloned.1.call-start = ((), (), s32[]{:S(2)}) async-start(), calls=%async_computation | async-start | bytes 8921088 | tf_op jit(solution)/shard_map/all_gather | solution.py:266
  10.8 202.6 %all-gather.7.cloned.1.call-start = ((), (), s32[]{:S(2)}) async-start(), calls=%async_computation.1 | async-start | bytes 16625664 | tf_op jit(solution)/shard_map/all_gather | solution.py:267
  13.9 37.7 %collective-permute-start = (bf16[512,1024]{1,0:T(8,128)(2,1)S(1)}, bf16[512,1024]{1,0:T(8,128)(2,1)S(1)}, u32[]{:S(2)}, u32[]{:S(2)}) collective-permute-start(bf16[512,1024]{1,0:T(8,128)(2,1)S(1)} %copy-done.15), channel_id=1, source_target_pairs={{0,1},{1,2},{2,3},{4,5},{5,6},{6,7},{8,9},{9,10},{10,11},{12,13},{... | collective-permute-start | bytes 3145736 | tf_op jit(solution)/shard_map/ppermute | solution.py:296
  18.9 41.1 %collective-permute-start.1 = (bf16[512,1024]{1,0:T(8,128)(2,1)S(1)}, bf16[512,1024]{1,0:T(8,128)(2,1)S(1)}, u32[]{:S(2)}, u32[]{:S(2)}) collective-permute-start(bf16[512,1024]{1,0:T(8,128)(2,1)S(1)} %copy-done.15), channel_id=1, source_target_pairs={{1,0},{2,1},{3,2},{5,4},{6,5},{7,6},{9,8},{10,9},{11,10},{13,12},{... | collective-permute-start | bytes 3145736 | tf_op jit(solution)/shard_map/ppermute | solution.py:297
  432.5 144.6 %collective-permute-start.24 = (bf16[4,2,2,128,656]{3,4,2,1,0:T(8,128)(2,1)}, bf16[4,2,2,128,656]{3,4,2,1,0:T(8,128)(2,1)}, u32[]{:S(2)}, u32[]{:S(2)}) collective-permute-start(bf16[4,2,2,128,656]{3,4,2,1,0:T(8,128)(2,1)} %bitcast.461), channel_id=1, source_target_pairs={{0,4},{4,0},{8,12},{12,8},{16,20},{20,16},{24,28},{28,24},{1,5},{5... | collective-permute-start | bytes 8060936 | tf_op jit(solution)/shard_map/ppermute | solution.py:189
  461.4 120.0 %collective-permute-start.14 = (bf16[4,2,2,128,656]{3,4,2,1,0:T(8,128)(2,1)}, bf16[4,2,2,128,656]{3,4,2,1,0:T(8,128)(2,1)}, u32[]{:S(2)}, u32[]{:S(2)}) collective-permute-start(bf16[4,2,2,128,656]{3,4,2,1,0:T(8,128)(2,1)} %bitcast.463), channel_id=1, source_target_pairs={{0,4},{4,0},{8,12},{12,8},{16,20},{20,16},{24,28},{28,24},{1,5},{5... | collective-permute-start | bytes 8060936 | tf_op jit(solution)/shard_map/ppermute | solution.py:189
  490.3 113.3 %collective-permute-start.19 = (bf16[4,2,2,128,656]{3,4,2,1,0:T(8,128)(2,1)}, bf16[4,2,2,128,656]{3,4,2,1,0:T(8,128)(2,1)}, u32[]{:S(2)}, u32[]{:S(2)}) collective-permute-start(bf16[4,2,2,128,656]{3,4,2,1,0:T(8,128)(2,1)} %bitcast.462), channel_id=1, source_target_pairs={{0,4},{4,0},{8,12},{12,8},{16,20},{20,16},{24,28},{28,24},{1,5},{5... | collective-permute-start | bytes 8060936 | tf_op jit(solution)/shard_map/ppermute | solution.py:189
  526.6 25.4 %collective-permute-start.2 = (bf16[512,1024]{1,0:T(8,128)(2,1)S(1)}, bf16[512,1024]{1,0:T(8,128)(2,1)S(1)}, u32[]{:S(2)}, u32[]{:S(2)}) collective-permute-start(bf16[512,1024]{1,0:T(8,128)(2,1)S(1)} %get-tuple-element.146), channel_id=1, source_target_pairs={{0,1},{1,2},{2,3},{4,5},{5,6},{6,7},{8,9},{9,10},{10,11},{12,13},{... | collective-permute-start | bytes 3145736 | tf_op jit(solution)/shard_map/ppermute | solution.py:362
  529.3 27.2 %collective-permute-start.3 = (bf16[512,1024]{1,0:T(8,128)(2,1)S(1)}, bf16[512,1024]{1,0:T(8,128)(2,1)S(1)}, u32[]{:S(2)}, u32[]{:S(2)}) collective-permute-start(bf16[512,1024]{1,0:T(8,128)(2,1)S(1)} %get-tuple-element.147), channel_id=1, source_target_pairs={{1,0},{2,1},{3,2},{5,4},{6,5},{7,6},{9,8},{10,9},{11,10},{13,12},{... | collective-permute-start | bytes 3145736 | tf_op jit(solution)/shard_map/ppermute | solution.py:361
  552.0 21.2 %collective-permute-start.9 = (bf16[2,2,256,1024]{2,3,0,1:T(8,128)(2,1)}, bf16[2,2,256,1024]{2,3,0,1:T(8,128)(2,1)}, u32[]{:S(2)}, u32[]{:S(2)}) collective-permute-start(bf16[2,2,256,1024]{2,3,0,1:T(8,128)(2,1)} %fusion.46), channel_id=1, source_target_pairs={{0,4},{4,0},{8,12},{12,8},{16,20},{20,16},{24,28},{28,24},{1,5},{5... | collective-permute-start | bytes 6291464 | tf_op jit(solution)/shard_map/ppermute | solution.py:189
  566.8 64.2 %collective-permute-start.4 = (bf16[2,2,272,1024]{3,2,1,0:T(8,128)(2,1)}, bf16[2,2,272,1024]{3,2,1,0:T(8,128)(2,1)}, u32[]{:S(2)}, u32[]{:S(2)}) collective-permute-start(bf16[2,2,272,1024]{3,2,1,0:T(8,128)(2,1)} %dynamic-slice_bitcast_fusion), channel_id=1, source_target_pairs={{0,4},{4,0},{8,12},{12,8},{16,20},{20,16},{24,28},{28,24},{1,5},{5... | collective-permute-start | bytes 6684680 | tf_op jit(solution)/shard_map/ppermute | solution.py:189
  575.6 26.2 %collective-permute-start.10 = (bf16[2,256,1024]{1,2,0:T(8,128)(2,1)S(1)}, bf16[2,256,1024]{1,2,0:T(8,128)(2,1)S(1)}, u32[]{:S(2)}, u32[]{:S(2)}) collective-permute-start(bf16[2,256,1024]{1,2,0:T(8,128)(2,1)S(1)} %dynamic-slice_bitcast_fusion.5), channel_id=1, source_target_pairs={{0,8},{4,12},{8,0},{12,4},{16,24},{20,28},{24,16},{28,20},{1,9},{5... | collective-permute-start | bytes 3145736 | tf_op jit(solution)/shard_map/ppermute | solution.py:189
  580.7 58.9 %collective-permute-start.25 = (bf16[4,2,128,656]{2,3,1,0:T(8,128)(2,1)}, bf16[4,2,128,656]{2,3,1,0:T(8,128)(2,1)}, u32[]{:S(2)}, u32[]{:S(2)}) collective-permute-start(bf16[4,2,128,656]{2,3,1,0:T(8,128)(2,1)} %dynamic-slice_bitcast_fusion.1), channel_id=1, source_target_pairs={{0,8},{4,12},{8,0},{12,4},{16,24},{20,28},{24,16},{28,20},{1,9},{5... | collective-permute-start | bytes 4030472 | tf_op jit(solution)/shard_map/ppermute | solution.py:189
  585.2 56.9 %collective-permute-start.15 = (bf16[4,2,128,656]{2,3,1,0:T(8,128)(2,1)}, bf16[4,2,128,656]{2,3,1,0:T(8,128)(2,1)}, u32[]{:S(2)}, u32[]{:S(2)}) collective-permute-start(bf16[4,2,128,656]{2,3,1,0:T(8,128)(2,1)} %dynamic-slice_bitcast_fusion.3), channel_id=1, source_target_pairs={{0,16},{4,20},{8,24},{12,28},{16,0},{20,4},{24,8},{28,12},{1,17},{... | collective-permute-start | bytes 4030472 | tf_op jit(solution)/shard_map/ppermute | solution.py:189
  602.1 24.5 %collective-permute-start.11 = (bf16[256,1024]{0,1:T(8,128)(2,1)S(1)}, bf16[256,1024]{0,1:T(8,128)(2,1)S(1)}, u32[]{:S(2)}, u32[]{:S(2)}) collective-permute-start(bf16[256,1024]{0,1:T(8,128)(2,1)S(1)} %dynamic-slice_bitcast_fusion.10), channel_id=1, source_target_pairs={{0,16},{4,20},{8,24},{12,28},{16,0},{20,4},{24,8},{28,12},{1,17},{... | collective-permute-start | bytes 1572872 | tf_op jit(solution)/shard_map/ppermute | solution.py:189
  608.6 50.8 %collective-permute-start.20 = (bf16[4,2,128,656]{2,3,1,0:T(8,128)(2,1)}, bf16[4,2,128,656]{2,3,1,0:T(8,128)(2,1)}, u32[]{:S(2)}, u32[]{:S(2)}) collective-permute-start(bf16[4,2,128,656]{2,3,1,0:T(8,128)(2,1)} %dynamic-slice_bitcast_fusion.2), channel_id=1, source_target_pairs={{0,8},{4,12},{8,0},{12,4},{16,24},{20,28},{24,16},{28,20},{1,9},{5... | collective-permute-start | bytes 4030472 | tf_op jit(solution)/shard_map/ppermute | solution.py:189
  636.7 32.8 %collective-permute-start.5 = (bf16[2,272,1024]{2,1,0:T(8,128)(2,1)}, bf16[2,272,1024]{2,1,0:T(8,128)(2,1)}, u32[]{:S(2)}, u32[]{:S(2)}) collective-permute-start(bf16[2,272,1024]{2,1,0:T(8,128)(2,1)} %dynamic-slice_bitcast_fusion.4), channel_id=1, source_target_pairs={{0,16},{4,20},{8,24},{12,28},{16,0},{20,4},{24,8},{28,12},{1,17},{... | collective-permute-start | bytes 3342344 | tf_op jit(solution)/shard_map/ppermute | solution.py:189
  639.6 24.9 %collective-permute-start.13 = (bf16[256,256]{1,0:T(8,128)(2,1)S(1)}, bf16[256,256]{1,0:T(8,128)(2,1)S(1)}, u32[]{:S(2)}, u32[]{:S(2)}) collective-permute-start(bf16[256,256]{1,0:T(8,128)(2,1)S(1)} %dynamic-slice_bitcast_fusion.20), channel_id=1, source_target_pairs={{0,2},{1,3},{2,0},{3,1},{4,6},{5,7},{6,4},{7,5},{8,10},{9,11},{10,... | collective-permute-start | bytes 393224 | tf_op jit(solution)/shard_map/ppermute | solution.py:189
  641.5 37.5 %collective-permute-start.26 = (bf16[4,128,656]{1,2,0:T(8,128)(2,1)S(1)}, bf16[4,128,656]{1,2,0:T(8,128)(2,1)}, u32[]{:S(2)}, u32[]{:S(2)}) collective-permute-start(bf16[4,128,656]{1,2,0:T(8,128)(2,1)S(1)} %dynamic-slice_bitcast_fusion.6), channel_id=1, source_target_pairs={{0,16},{4,20},{8,24},{12,28},{16,0},{20,4},{24,8},{28,12},{1,17},{... | collective-permute-start | bytes 2015240 | tf_op jit(solution)/shard_map/ppermute | solution.py:189
  645.4 36.0 %collective-permute-start.16 = (bf16[4,128,656]{1,2,0:T(8,128)(2,1)}, bf16[4,128,656]{1,2,0:T(8,128)(2,1)}, u32[]{:S(2)}, u32[]{:S(2)}) collective-permute-start(bf16[4,128,656]{1,2,0:T(8,128)(2,1)} %dynamic-slice_bitcast_fusion.8), channel_id=1, source_target_pairs={{0,8},{4,12},{8,0},{12,4},{16,24},{20,28},{24,16},{28,20},{1,9},{5... | collective-permute-start | bytes 2015240 | tf_op jit(solution)/shard_map/ppermute | solution.py:189
  663.1 26.7 %collective-permute-start.21 = (bf16[4,128,656]{1,2,0:T(8,128)(2,1)}, bf16[4,128,656]{1,2,0:T(8,128)(2,1)}, u32[]{:S(2)}, u32[]{:S(2)}) collective-permute-start(bf16[4,128,656]{1,2,0:T(8,128)(2,1)} %dynamic-slice_bitcast_fusion.7), channel_id=1, source_target_pairs={{0,16},{4,20},{8,24},{12,28},{16,0},{20,4},{24,8},{28,12},{1,17},{... | collective-permute-start | bytes 2015240 | tf_op jit(solution)/shard_map/ppermute | solution.py:189
  671.4 20.9 %collective-permute-start.6 = (bf16[272,1024]{1,0:T(8,128)(2,1)S(1)}, bf16[272,1024]{1,0:T(8,128)(2,1)S(1)}, u32[]{:S(2)}, u32[]{:S(2)}) collective-permute-start(bf16[272,1024]{1,0:T(8,128)(2,1)S(1)} %dynamic-slice_bitcast_fusion.9), channel_id=1, source_target_pairs={{0,8},{4,12},{8,0},{12,4},{16,24},{20,28},{24,16},{28,20},{1,9},{5... | collective-permute-start | bytes 1671176 | tf_op jit(solution)/shard_map/ppermute | solution.py:189
  693.1 27.7 %collective-permute-start.7 = (bf16[2,272,256]{2,1,0:T(8,128)(2,1)S(1)}, bf16[2,272,256]{2,1,0:T(8,128)(2,1)S(1)}, u32[]{:S(2)}, u32[]{:S(2)}) collective-permute-start(bf16[2,272,256]{2,1,0:T(8,128)(2,1)S(1)} %dynamic-slice_bitcast_fusion.14), channel_id=1, source_target_pairs={{0,1},{1,0},{2,3},{3,2},{4,5},{5,4},{6,7},{7,6},{8,9},{9,8},{10,11... | collective-permute-start | bytes 835592 | tf_op jit(solution)/shard_map/ppermute | solution.py:189
  694.8 26.2 %collective-permute-start.28 = (bf16[128,656]{0,1:T(8,128)(2,1)S(1)}, bf16[128,656]{0,1:T(8,128)(2,1)S(1)}, u32[]{:S(2)}, u32[]{:S(2)}) collective-permute-start(bf16[128,656]{0,1:T(8,128)(2,1)S(1)} %dynamic-slice_bitcast_fusion.16), channel_id=1, source_target_pairs={{0,2},{1,3},{2,0},{3,1},{4,6},{5,7},{6,4},{7,5},{8,10},{9,11},{10,... | collective-permute-start | bytes 503816 | tf_op jit(solution)/shard_map/ppermute | solution.py:189
  (91 other events, 1091.7 us)
Sparse Core Ops, SparseCore 0:
  11.4 88.1 all-gather.4
  103.0 110.4 all-gather.6
